TPU v7x, 128 devices: a whole 4x4x4 slice. The times are simulated.
128 devices in a mesh: row: 16 (over z, y), col: 8 (over x, core).
Axes of the slice: x: 4, y: 4, z: 4, core: 2. Of those that a mesh axis runs over, the one named last changes fastest.
Arguments:
- points: bfloat16 [24576, 256], P(('row', 'col')), may hold values from -0.5 to 0.5
- lengthscale: float32 [256], replicated, may hold values from 0.1 to 4
- solution_vals: float32 [24576], P(('row', 'col')), may hold values from -6 to 6
- solution_grads: float32 [24576, 256], P(('row', 'col')), may hold values from -6 to 6
- residual_vals: float32 [24576], P(('row', 'col')), may hold values from -80 to 80
- residual_grads: float32 [24576, 256], P(('row', 'col')), may hold values from -80 to 80
- direction_vals: float32 [24576], P(('row', 'col')), may hold values from -80 to 80
- direction_grads: float32 [24576, 256], P(('row', 'col')), may hold values from -80 to 80
Outputs:
- next_solution_vals: float32 [24576], P(('row', 'col'))
- next_solution_grads: float32 [24576, 256], P(('row', 'col'))
- next_residual_vals: float32 [24576], P(('row', 'col'))
- next_residual_grads: float32 [24576, 256], P(('row', 'col'))
- next_direction_vals: float32 [24576], P(('row', 'col'))
- next_direction_grads: float32 [24576, 256], P(('row', 'col'))
All inputs are finite; a program needn't handle non-finite values.
Results may differ from a plain program's by a relative error of at most 0.0038.
Values may be sent and summed in bfloat16 or wider, within the bound.
A program may use at most 64 MiB of HBM per device.

v0:
```python
import math

import jax
import jax.numpy as jnp
from jax import lax
from jax.sharding import PartitionSpec as P

nugget_level = 4.0


def contract(left, right):
    return lax.dot_general(
        left, right, (((1,), (1,)), ((), ())), preferred_element_type=jnp.float32
    )


def partial_terms(target_points, source_points, source_vals, source_grads):
    source_square = jnp.sum(jnp.square(source_points.astype(jnp.float32)), axis=1)
    source_shift = jnp.sum(
        source_points.astype(jnp.float32) * source_grads.astype(jnp.float32), axis=1
    )
    source_level = source_vals.astype(jnp.float32)
    row_count, width = target_points.shape
    block_size = math.gcd(row_count, 1024)

    def one_block(target_tile):
        target_square = jnp.sum(jnp.square(target_tile.astype(jnp.float32)), axis=1)
        distance = (
            target_square[:, None]
            + source_square[None, :]
            - 2.0 * contract(target_tile, source_points)
        )
        kernel = jnp.exp(-0.5 * distance)
        inner_terms = contract(target_tile, source_grads) - source_shift[None, :]
        weight = kernel * (source_level[None, :] + inner_terms)
        total_weight = jnp.sum(weight, axis=1)
        mixed_terms = jnp.dot(
            kernel.astype(jnp.bfloat16), source_grads, preferred_element_type=jnp.float32
        )
        mixed_terms = mixed_terms + jnp.dot(
            weight.astype(jnp.bfloat16), source_points, preferred_element_type=jnp.float32
        )
        return (total_weight, mixed_terms)

    tiles = target_points.reshape(row_count // block_size, block_size, width)
    total_weight, mixed_terms = lax.map(one_block, tiles)
    return (total_weight.reshape(row_count), mixed_terms.reshape(row_count, width))


def squared_norm(first_part, second_part):
    return jnp.sum(first_part * first_part) + jnp.sum(second_part * second_part)


def body(
    points,
    lengthscale,
    solution_vals,
    solution_grads,
    residual_vals,
    residual_grads,
    direction_vals,
    direction_grads,
):
    root_scale = jnp.sqrt(lengthscale)
    scaled = (points.astype(jnp.float32) * root_scale).astype(jnp.bfloat16)
    level_low = direction_vals.astype(jnp.bfloat16)
    slope_low = (direction_grads * root_scale).astype(jnp.bfloat16)
    source_vals, source_grads, source_points = (
        lax.all_gather(level_low, "col", axis=0, tiled=True),
        lax.all_gather(slope_low, "col", axis=0, tiled=True),
        lax.all_gather(scaled, "col", axis=0, tiled=True),
    )
    target_points = lax.all_gather(scaled, "row", axis=0, tiled=True)
    total_weight, mixed_terms = partial_terms(
        target_points, source_points, source_vals, source_grads
    )
    total_weight, mixed_terms = (
        lax.psum_scatter(total_weight, "row", scatter_dimension=0, tiled=True),
        lax.psum_scatter(mixed_terms, "row", scatter_dimension=0, tiled=True),
    )
    image_vals = total_weight + nugget_level * direction_vals
    image_grads = (
        root_scale * (mixed_terms - scaled.astype(jnp.float32) * total_weight[:, None])
        + nugget_level * direction_grads
    )
    norm_now = lax.psum(squared_norm(residual_vals, residual_grads), ("row", "col"))
    local_curve = jnp.sum(direction_vals * image_vals) + jnp.sum(direction_grads * image_grads)
    curvature = lax.psum(local_curve, ("row", "col"))
    step_size = norm_now / curvature
    next_residual_vals = residual_vals - step_size * image_vals
    next_residual_grads = residual_grads - step_size * image_grads
    norm_next = lax.psum(squared_norm(next_residual_vals, next_residual_grads), ("row", "col"))
    next_solution_vals = solution_vals + step_size * direction_vals
    next_solution_grads = solution_grads + step_size * direction_grads
    ratio_next = norm_next / norm_now
    next_direction_vals = next_residual_vals + ratio_next * direction_vals
    next_direction_grads = next_residual_grads + ratio_next * direction_grads
    return (
        next_solution_vals,
        next_solution_grads,
        next_residual_vals,
        next_residual_grads,
        next_direction_vals,
        next_direction_grads,
    )


def solution(mesh):
    return jax.shard_map(
        body,
        mesh=mesh,
        in_specs=(
            P(("row", "col"), None),
            P(),
            P(("row", "col")),
            P(("row", "col"), None),
            P(("row", "col")),
            P(("row", "col"), None),
            P(("row", "col")),
            P(("row", "col"), None),
        ),
        out_specs=(
            P(("row", "col")),
            P(("row", "col"), None),
            P(("row", "col")),
            P(("row", "col"), None),
            P(("row", "col")),
            P(("row", "col"), None),
        ),
        check_vma=False,
    )
```

profile of v0, /device:TPU:1, one launch (start us, length us, event | category | flops | bytes accessed | tf_op | source)
XLA Modules:
  0.0 321.7 jit_solution(9862147485114120289)
XLA Ops:
  7.2 0.0 all-gather.2.cloned.1.call-start
  7.2 0.7 sqrt.3
  7.9 1.7 multiply_convert_fusion
  9.6 0.0 all-gather.2.cloned.1.call-update
  9.6 0.0 reduce-scatter.2.cloned.1.call-start
  9.7 0.7 convert_element_type.37
  10.3 1.2 dynamic-slice
  12.2 0.2 dynamic-update-slice
  12.5 13.2 %all-reduce = bf16[1536]{0:T(1024)(128)(2,1)S(1)} all-reduce(bf16[1536]{0:T(1024)(128)(2,1)S(1)} %dynamic-update-slice), channel_id=1, replica_groups=mesh['row'=16,'col'=8] {'col'}, use_global_device_ids=true, to_apply=%add | all-reduce | flops 1536 | bytes 6144
  25.7 16.4 %all_gather.13 = bf16[1536,256]{1,0:T(8,128)(2,1)S(1)} all-gather(bf16[192,256]{1,0:T(8,128)(2,1)} %get-tuple-element.91), channel_id=1, replica_groups=mesh['row'=16,'col'=8] {'col'}, dimensions={0}, use_global_device_ids=true | all-gather | bytes 884736 | tf_op jit(solution)/shard_map/all_gather | solution.py:71
  42.1 13.5 %all_gather.15 = bf16[1536,256]{1,0:T(8,128)(2,1)S(1)} all-gather(bf16[192,256]{1,0:T(8,128)(2,1)S(1)} %get-tuple-element.90), channel_id=1, replica_groups=mesh['row'=16,'col'=8] {'col'}, dimensions={0}, use_global_device_ids=true | all-gather | bytes 884736 | tf_op jit(solution)/shard_map/all_gather | solution.py:70
  55.6 0.5 fusion.20
  56.1 1.0 all-gather.2.cloned.1.call-done
  57.1 42.1 %while.12 = (s32[]{:T(128)}, f32[3,1024]{1,0:T(4,128)S(1)}, f32[3,1024,256]{2,1,0:T(8,128)}, bf16[3,1024,256]{2,1,0:T(8,128)(2,1)}, f32[1536]{0:T(1024)S(1)}, /*...) while((s32[]{:T(128)}, f32[3,1024]{1,0:T(4,128)S(1)}, ...), condition=%wide.region_8.9_spmd, body=%wide.region_5.8_spmd.sunk | while | flops 3238000640 | bytes 83400896 | solution.py:46
  57.1 1.3 multiply_reduce_fusion.8
  58.4 2.5 multiply_exponential_fusion.2
  60.9 0.0 copy-start
  60.9 4.4 %fusion.44 = (f32[1024]{0:T(1024)S(1)}, bf16[1024,1536]{1,0:T(8,128)(2,1)}) fusion(f32[1024,1536]{1,0:T(8,128)S(1)} %multiply_exponential_fusion.2, f32[1536]{0:T(1024)S(1)} %get-tuple-element.183, bf16[1536,256]{1,0:T(8,128)(2,1)S(1)} %get-tuple-element.182, bf16[3,1024,256]{2,1,0:T(8,128)(2,1)} %get-tuple-element.178, s32[]{:T(128)S(6)} %copy.20, ...), kind=kOutput, calls=%fused_computation.36.clone.1 | convolution fusion | flops 813169664 | bytes 10764292 | tf_op jit(solution)/shard_map/while/body/eval_jaxpr/dot_general | solution.py:12
  65.3 0.0 copy-done
  65.4 0.0 copy-start.1
  65.4 3.0 fusion.45
  68.4 0.7 copy-done.1
  69.1 2.0 fusion.46
  71.1 1.3 multiply_reduce_fusion.8
  72.4 2.5 multiply_exponential_fusion.2
  74.9 0.0 copy-start
  74.9 4.4 %fusion.44 = (f32[1024]{0:T(1024)S(1)}, bf16[1024,1536]{1,0:T(8,128)(2,1)}) fusion(f32[1024,1536]{1,0:T(8,128)S(1)} %multiply_exponential_fusion.2, f32[1536]{0:T(1024)S(1)} %get-tuple-element.183, bf16[1536,256]{1,0:T(8,128)(2,1)S(1)} %get-tuple-element.182, bf16[3,1024,256]{2,1,0:T(8,128)(2,1)} %get-tuple-element.178, s32[]{:T(128)S(6)} %copy.20, ...), kind=kOutput, calls=%fused_computation.36.clone.1 | convolution fusion | flops 813169664 | bytes 10764292 | tf_op jit(solution)/shard_map/while/body/eval_jaxpr/dot_general | solution.py:12
  79.4 0.0 copy-done
  79.4 0.0 copy-start.1
  79.4 3.0 fusion.45
  82.5 0.7 copy-done.1
  83.2 2.0 fusion.46
  85.1 1.3 multiply_reduce_fusion.8
  86.4 2.5 multiply_exponential_fusion.2
  88.9 0.0 copy-start
  88.9 4.4 %fusion.44 = (f32[1024]{0:T(1024)S(1)}, bf16[1024,1536]{1,0:T(8,128)(2,1)}) fusion(f32[1024,1536]{1,0:T(8,128)S(1)} %multiply_exponential_fusion.2, f32[1536]{0:T(1024)S(1)} %get-tuple-element.183, bf16[1536,256]{1,0:T(8,128)(2,1)S(1)} %get-tuple-element.182, bf16[3,1024,256]{2,1,0:T(8,128)(2,1)} %get-tuple-element.178, s32[]{:T(128)S(6)} %copy.20, ...), kind=kOutput, calls=%fused_computation.36.clone.1 | convolution fusion | flops 813169664 | bytes 10764292 | tf_op jit(solution)/shard_map/while/body/eval_jaxpr/dot_general | solution.py:12
  93.4 0.0 copy-done
  93.4 0.0 copy-start.1
  93.4 3.0 fusion.45
  96.5 0.7 copy-done.1
  97.2 2.1 fusion.46
  99.2 0.0 copy-start.2
  99.2 0.0 copy-start.3
  99.3 0.0 copy-start.10
  99.3 0.0 copy-start.6
  99.3 0.0 reduce-scatter.2.cloned.1.call-update
  99.3 0.6 copy-done.11
  99.9 0.6 dynamic-slice.1
  101.1 0.0 copy-done.9
  101.1 0.6 multiply_reduce_fusion.6
  101.7 0.0 copy-done.4
  101.7 0.6 multiply_reduce_fusion.3
  103.7 61.2 %all-reduce.1 = f32[3072]{0:T(1024)S(1)} all-reduce(f32[3072]{0:T(1024)S(1)} %reshape.28), channel_id=2, replica_groups=mesh['row'=16,'col'=8] {'row'}, use_global_device_ids=true, to_apply=%region_9.10.clone | all-reduce | flops 3072 | bytes 24576
  164.9 0.7 multiply_reduce_fusion.5
  165.6 8.4 %reduce-scatter.2.cloned.1.call-done = f32[192,256]{1,0:T(8,128)} async-done(((f32[3072,256]{1,0:T(8,128)}), f32[192,256]{1,0:T(8,128)}) %reduce-scatter.2.cloned.1.call-update) | async-done | bytes 196624 | tf_op jit(solution)/shard_map/reduce_scatter | solution.py:79
  173.9 1.7 multiply_reduce_fusion.2
  176.9 67.1 %all-reduce.2 = (f32[]{:T(128)}, f32[]{:T(128)}) all-reduce(f32[]{:T(128)S(6)} %add.64, f32[]{:T(128)S(6)} %add.67), channel_id=1, replica_groups=mesh['row'=16,'col'=8] {'row','col'}, use_global_device_ids=true, to_apply=%region_2.3 | all-reduce | flops 2 | bytes 16 | tf_op jit(solution)/shard_map/psum | solution.py:86
  245.3 0.6 multiply_reduce_fusion.4
  246.0 1.7 multiply_reduce_fusion.1
  248.9 63.2 %psum.23 = f32[]{:T(128)} all-reduce(f32[]{:T(128)S(6)} %add.70), channel_id=1, replica_groups=mesh['row'=16,'col'=8] {'row','col'}, use_global_device_ids=true, to_apply=%region_16.17 | all-reduce | flops 1 | bytes 8 | tf_op jit(solution)/shard_map/psum | solution.py:92
  313.5 0.6 multiply_add_fusion.3
  314.0 0.0 copy-done.6
  314.0 0.8 multiply_add_fusion
  314.8 0.0 copy-done.5
  (19 shorter events, 0.2 us)
Async XLA Ops:
  7.2 49.9 %all-gather.2.cloned.1.call-start = ((), (), s32[]{:S(2)}) async-start(), calls=%async_computation.1 | async-start | bytes 1671168 | tf_op jit(solution)/shard_map/all_gather | solution.py:73
  9.6 164.3 %reduce-scatter.2.cloned.1.call-start = ((), (), s32[]{:S(2)}) async-start(), calls=%async_computation.2 | async-start | bytes 3342336 | tf_op jit(solution)/shard_map/reduce_scatter | solution.py:79
  60.9 4.4 %copy-start = (f32[1024,1536]{1,0:T(8,128)}, f32[1024,1536]{1,0:T(8,128)S(1)}, u32[]{:S(2)}) copy-start(f32[1024,1536]{1,0:T(8,128)S(1)} %multiply_exponential_fusion.2) | copy-start | bytes 18874372 | tf_op jit(solution)/shard_map/while
  65.4 3.7 %copy-start.1 = (f32[1024,1536]{1,0:T(8,128)S(1)}, f32[1024,1536]{1,0:T(8,128)}, u32[]{:S(2)}) copy-start(f32[1024,1536]{1,0:T(8,128)} %copy-done) | copy-start | bytes 18874372 | tf_op jit(solution)/shard_map/while
  74.9 4.4 %copy-start = (f32[1024,1536]{1,0:T(8,128)}, f32[1024,1536]{1,0:T(8,128)S(1)}, u32[]{:S(2)}) copy-start(f32[1024,1536]{1,0:T(8,128)S(1)} %multiply_exponential_fusion.2) | copy-start | bytes 18874372 | tf_op jit(solution)/shard_map/while
  79.4 3.7 %copy-start.1 = (f32[1024,1536]{1,0:T(8,128)S(1)}, f32[1024,1536]{1,0:T(8,128)}, u32[]{:S(2)}) copy-start(f32[1024,1536]{1,0:T(8,128)} %copy-done) | copy-start | bytes 18874372 | tf_op jit(solution)/shard_map/while
  88.9 4.4 %copy-start = (f32[1024,1536]{1,0:T(8,128)}, f32[1024,1536]{1,0:T(8,128)S(1)}, u32[]{:S(2)}) copy-start(f32[1024,1536]{1,0:T(8,128)S(1)} %multiply_exponential_fusion.2) | copy-start | bytes 18874372 | tf_op jit(solution)/shard_map/while
  93.4 3.7 %copy-start.1 = (f32[1024,1536]{1,0:T(8,128)S(1)}, f32[1024,1536]{1,0:T(8,128)}, u32[]{:S(2)}) copy-start(f32[1024,1536]{1,0:T(8,128)} %copy-done) | copy-start | bytes 18874372 | tf_op jit(solution)/shard_map/while
  99.2 0.7 copy-start.11
  99.2 1.9 copy-start.9
  99.2 2.5 copy-start.4
  99.2 65.7 %copy-start.7 = (f32[192]{0:T(256)S(1)}, f32[192]{0:T(256)}, u32[]{:S(2)}) copy-start(f32[192]{0:T(256)} %param.16) | copy-start | bytes 2308
  99.2 74.7 %copy-start.2 = (f32[192,256]{1,0:T(8,128)S(1)}, f32[192,256]{1,0:T(8,128)}, u32[]{:S(2)}) copy-start(f32[192,256]{1,0:T(8,128)} %param.17) | copy-start | bytes 589828
  99.2 74.7 %copy-start.3 = (bf16[192,256]{1,0:T(8,128)(2,1)S(1)}, bf16[192,256]{1,0:T(8,128)(2,1)}, u32[]{:S(2)}) copy-start(bf16[192,256]{1,0:T(8,128)(2,1)} %param.10) | copy-start | bytes 294916
  99.3 214.2 %copy-start.10 = (f32[192]{0:T(256)S(1)}, f32[192]{0:T(256)}, u32[]{:S(2)}) copy-start(f32[192]{0:T(256)} %param.12) | copy-start | bytes 2308
  99.3 214.8 %copy-start.6 = (f32[192,256]{1,0:T(8,128)S(1)}, f32[192,256]{1,0:T(8,128)}, u32[]{:S(2)}) copy-start(f32[192,256]{1,0:T(8,128)} %param.13) | copy-start | bytes 589828
  245.9 68.9 %copy-start.8 = (f32[192]{0:T(256)}, f32[192]{0:T(256)S(1)}, u32[]{:S(2)}) copy-start(f32[192]{0:T(256)S(1)} %get-tuple-element.81) | copy-start | bytes 2308
  247.6 67.2 %copy-start.5 = (f32[192,256]{1,0:T(8,128)}, f32[192,256]{1,0:T(8,128)S(1)}, u32[]{:S(2)}) copy-start(f32[192,256]{1,0:T(8,128)S(1)} %get-tuple-element.79) | copy-start | bytes 589828
Sparse Core Ops, SparseCore 0:
  10.7 46.3 all-gather.1
  99.4 74.4 reduce-scatter.1
where the time goes:
time: 323 us; the launch traced here: 322 us
  blocking collectives  235 us (73%)
  matrix products  36 us (11%)
  between operations  22 us (7%)
  other arithmetic  13.8 us (4%)
  waiting for transfers between devices  9.42 us (3%)
  local copies, waits for them, and re-layouts  5.65 us (2%)
    unnamed x2, blocking collectives  74.4 us
    psum x1, blocking collectives, body(): lax.psum(squared_norm(residual_vals, residual_grads), ('row', 'col'))  67.1 us
    psum x1, blocking collectives, body(): lax.psum(squared_norm(next_residual_vals, next_residual_grads), ('row', '...  63.2 us
    dot_general x6, matrix products, contract(): lax.dot_general(left, right, (((1,), (1,)), ((), ())), preferred_element_...  20.9 us
    all_gather x1, blocking collectives, body(): lax.all_gather(scaled, 'col', axis=0, tiled=True)  16.4 us
    all_gather x1, blocking collectives, body(): lax.all_gather(slope_low, 'col', axis=0, tiled=True)  13.5 us
    dot_general x3, matrix products, one_block(): jnp.dot(weight.astype(jnp.bfloat16), source_points, preferred_element_typ...  9.04 us
    reduce_scatter x1, waiting for transfers between devices, body(): lax.psum_scatter(mixed_terms, 'row', scatter_dimension=0, tiled=True)  8.35 us
  transfers between devices with their start and end apart: 2, of which 2 were waited for; matrix products, arithmetic and copies ran while one was open for 2% of the time, Pallas kernels for 0%

commit v1 on v0

v1 whole, which is shorter than its diff:
```python
import functools
import math

import jax
import jax.numpy as jnp
from jax import lax
from jax.experimental import pallas as pl
from jax.experimental.pallas import tpu as pltpu
from jax.sharding import PartitionSpec as P

MESH = pl.DeviceIdType.MESH
LOG2E = math.log2(math.e)
NUGGET = 4.0
RING = 4
ROWS = 192
DIM = 256
LANES = 128
TAIL = ROWS - LANES
X_ROWS = 2 * ROWS
S_ROWS = 2 * ROWS
V_ROWS = 16
BLOCK = X_ROWS + S_ROWS + V_ROWS
CUT = X_ROWS
OFFSETS = (0, 1, 3, 2)
COUNT = 128


def slot_of(f, s):
    fi, si = OFFSETS.index(f % RING), OFFSETS.index(s % RING)
    return fi if si == 0 else 4 + 3 * fi + si - 1


def target_slot(t, k):
    return 2 * OFFSETS.index(t % RING) + k


def kernel(
    points_ref,
    scale_ref,
    sv_ref,
    sg_ref,
    rv_ref,
    rg_ref,
    dv_ref,
    dg_ref,
    nsv_ref,
    nsg_ref,
    nrv_ref,
    nrg_ref,
    ndv_ref,
    ndg_ref,
    slots,
    tx,
    ta,
    acc,
    tot,
    part,
    ptot,
    rsb,
    rst,
    vecs,
    mine,
    arb,
    g_send,
    g_recv,
    x_send,
    x_recv,
    r_send,
    r_recv,
    p_send,
    p_recv,
    a_send,
    a_recv,
):
    row, col = lax.axis_index("row"), lax.axis_index("col")
    z, y = row // RING, row % RING
    x, c = col // 2, col % 2
    o = 1 - c

    def first(d):
        return (z * RING + (y + d) % RING, col)

    def second(d, core):
        return (((z + o * d) % RING) * RING + y, ((x + c * d) % RING) * 2 + core)

    def third(d, core):
        return (((z + c * d) % RING) * RING + y, ((x + o * d) % RING) * 2 + core)

    barrier = pltpu.get_barrier_semaphore()
    near = [first(1), first(3), second(1, c), second(3, c)]
    near += [third(t, c) for t in (1, 2, 3)] + [third(t, o) for t in range(RING)]
    near += [second(t, o) for t in (1, 2, 3)]
    for peer in near:
        pl.semaphore_signal(barrier, inc=1, device_id=peer, device_id_type=MESH)

    root = jnp.sqrt(scale_ref[...])
    scaled = (points_ref[...].astype(jnp.float32) * root).astype(jnp.bfloat16)
    slope = (dg_ref[...] * root).astype(jnp.bfloat16)
    for p in range(2):
        lanes = slice(p * LANES, (p + 1) * LANES)
        slots[0, p * ROWS : (p + 1) * ROWS, :] = scaled[:, lanes]
        slots[0, X_ROWS + p * ROWS : X_ROWS + (p + 1) * ROWS, :] = slope[:, lanes]
        tx[0, p * ROWS : (p + 1) * ROWS, :] = scaled[:, lanes]
    wide = scaled.astype(jnp.float32)
    square = jnp.sum(wide * wide, axis=1, keepdims=True)
    shift = jnp.sum(wide * slope.astype(jnp.float32), axis=1, keepdims=True)
    lane = lax.broadcasted_iota(jnp.int32, (ROWS, LANES), 1)
    both = jnp.where(lane == 0, square, jnp.where(lane == 1, shift, 0.0))
    both = jnp.concatenate([both, both[LANES:]], axis=0)
    across = both.T
    level = dv_ref[...].astype(jnp.bfloat16).astype(jnp.float32)
    base = across[0:1] * (-0.5 * LOG2E)
    terms = (
        base[:, :LANES],
        base[:, LANES:],
        level[:, :LANES] - across[1:2, :LANES],
        jnp.concatenate([level[:, LANES:], level[:, LANES:]], axis=1) - across[1:2, LANES:],
    )
    vecs[...] = jnp.zeros_like(vecs)
    for i, term in enumerate(terms):
        for j in range(3):
            piece = term.astype(jnp.bfloat16).astype(jnp.float32)
            vecs[3 * i + j : 3 * i + j + 1, :] = piece
            term = term - piece
    slots[0, X_ROWS + S_ROWS :, :] = vecs[...].astype(jnp.bfloat16)

    copies = {}

    def describe(f, s, half, source, peer):
        n = len(copies)
        where = {None: slice(0, BLOCK), 0: slice(0, CUT), 1: slice(CUT, BLOCK)}[half]
        rows = pl.ds(where.start, where.stop - where.start)
        copies[f, s, half] = pltpu.make_async_remote_copy(
            src_ref=slots.at[slot_of(*source), rows],
            dst_ref=slots.at[slot_of(f, s), rows],
            send_sem=g_send.at[n],
            recv_sem=g_recv.at[n],
            device_id=peer,
            device_id_type=MESH,
        )

    describe(1, 0, None, (0, 0), first(3))
    describe(3, 0, None, (0, 0), first(1))
    describe(2, 0, 0, (3, 0), first(1))
    describe(2, 0, 1, (1, 0), first(3))
    for f in OFFSETS:
        describe(f, 1, None, (f, 0), second(3, c))
        describe(f, 3, None, (f, 0), second(1, c))
        describe(f, 2, 0, (f, 3), second(1, c))
        describe(f, 2, 1, (f, 1), second(3, c))

    x_copies, r_copies, p_copies = {}, {}, {}
    for t in OFFSETS:
        for k in range(2):
            if (t, k) == (0, 0):
                continue
            n = target_slot(t, k)
            back = (RING - t) % RING
            x_copies[t, k] = pltpu.make_async_remote_copy(
                src_ref=slots.at[0, pl.ds(0, X_ROWS)],
                dst_ref=tx.at[n],
                send_sem=x_send.at[n],
                recv_sem=x_recv.at[n],
                device_id=second(back, o) if k else third(back, c),
                device_id_type=MESH,
            )
            owner = third(back, o) if k else third(back, c)
            r_copies[t, k] = pltpu.make_async_remote_copy(
                src_ref=part.at[target_slot(back, k)],
                dst_ref=rsb.at[n],
                send_sem=r_send.at[n],
                recv_sem=r_recv.at[n],
                device_id=owner,
                device_id_type=MESH,
            )
            p_copies[t, k] = pltpu.make_async_remote_copy(
                src_ref=ptot.at[target_slot(back, k)],
                dst_ref=rst.at[n],
                send_sem=p_send.at[n],
                recv_sem=p_recv.at[n],
                device_id=owner,
                device_id_type=MESH,
            )

    def tile_points(i):
        planes = []
        for p in range(2):
            rows = slice(p * ROWS, (p + 1) * ROWS)
            planes.append(jnp.concatenate([tx[2 * i, rows, :], tx[2 * i + 1, rows, :]], axis=0))
        return jnp.concatenate(planes, axis=1)

    def target_base(i):
        value = tile_points(i).astype(jnp.float32)
        total = jnp.sum(value * value, axis=1, keepdims=True) * (-0.5 * LOG2E)
        ta[i] = jnp.broadcast_to(total, (2 * ROWS, LANES))

    low = lax.broadcasted_iota(jnp.int32, (1, LANES), 1) < TAIL

    def sources(g):
        held = range(4 * g, 4 * g + 4)

        def plane(p):
            top = p * ROWS
            pieces = [slots[s, top : top + LANES, :] for s in held]
            pieces += [slots[s, top + LANES : top + ROWS, :] for s in held]
            return jnp.concatenate(pieces, axis=0)

        xs = jnp.concatenate([plane(0), plane(1)], axis=1)
        ss = jnp.concatenate([plane(2), plane(3)], axis=1)

        def vector(i):
            heads, tails = [], []
            for s in held:
                v = slots[s, X_ROWS + S_ROWS :, :].astype(jnp.float32)
                heads.append(v[3 * i : 3 * i + 1] + v[3 * i + 1 : 3 * i + 2] + v[3 * i + 2 : 3 * i + 3])
                j = 3 * i + 3
                tails.append(v[j : j + 1] + v[j + 1 : j + 2] + v[j + 2 : j + 3])
            heads.append(jnp.where(low, tails[0], tails[1]))
            heads.append(jnp.where(low, tails[2], tails[3]))
            return jnp.concatenate(heads, axis=1)

        return xs, ss, vector(0), vector(2)

    def contract(left, right):
        return lax.dot_general(
            left, right, (((1,), (1,)), ((), ())), preferred_element_type=jnp.float32
        )

    def tile_terms(g, loaded, i):
        xs, ss, sb, sc = loaded
        points = tile_points(i)
        base = jnp.concatenate([ta[i]] * 6, axis=1)
        kern = jnp.exp2(contract(points, xs) * LOG2E + (base + sb))
        weight = kern * (contract(points, ss) + sc)
        total = weight[:, :LANES]
        for q in range(1, 6):
            total = total + weight[:, q * LANES : (q + 1) * LANES]
        pair = jnp.concatenate([kern.astype(jnp.bfloat16), weight.astype(jnp.bfloat16)], axis=1)
        mixed = jnp.dot(
            pair, jnp.concatenate([ss, xs], axis=0), preferred_element_type=jnp.float32
        )
        if g > 0:
            mixed, total = mixed + acc[i], total + tot[i]
        return mixed, total

    def compute(g, tiles):
        loaded = sources(g)
        for i in tiles:
            mixed, total = tile_terms(g, loaded, i)
            acc[i] = mixed
            tot[i] = total

    pl.semaphore_wait(barrier, len(near))
    copies[1, 0, None].start()
    copies[3, 0, None].start()
    x_copies[0, 1].start()
    for t in (2, 1, 3):
        x_copies[t, 0].start()
        x_copies[t, 1].start()
    copies[0, 1, None].start()
    copies[0, 3, None].start()

    copies[3, 0, None].wait_recv()
    copies[2, 0, 0].start()
    copies[1, 0, None].wait_recv()
    copies[2, 0, 1].start()
    for f in (1, 3):
        copies[f, 1, None].start()
        copies[f, 3, None].start()

    def relay(f):
        copies[f, 3, None].wait_recv()
        copies[f, 2, 0].start()
        copies[f, 1, None].wait_recv()
        copies[f, 2, 1].start()

    def settle(f):
        copies[f, 2, 0].wait_recv()
        copies[f, 2, 1].wait_recv()

    x_copies[0, 1].wait_recv()
    target_base(0)
    for i, t in ((1, 1), (2, 3)):
        x_copies[t, 0].wait_recv()
        x_copies[t, 1].wait_recv()
        target_base(i)
    settle_first = (copies[2, 0, 0], copies[2, 0, 1])
    for copy in settle_first:
        copy.wait_recv()
    copies[2, 1, None].start()
    copies[2, 3, None].start()

    compute(0, (0, 1))
    relay(0)
    x_copies[2, 0].wait_recv()
    x_copies[2, 1].wait_recv()
    target_base(3)
    compute(0, (2, 3))
    relay(1)
    settle(0)
    compute(1, (0, 1))
    relay(3)
    compute(1, (2, 3))
    settle(1)
    compute(2, (0, 1))
    relay(2)
    compute(2, (2, 3))
    settle(3)
    settle(2)

    loaded = sources(3)
    for i in (3, 1, 2, 0):
        mixed, total = tile_terms(3, loaded, i)
        total = jnp.sum(total, axis=1, keepdims=True)
        mixed = mixed - tile_points(i).astype(jnp.float32) * total
        for k in range(2):
            n = 2 * i + k
            rows = slice(k * ROWS, (k + 1) * ROWS)
            line = jnp.broadcast_to(total[rows], (ROWS, LANES))
            line = jnp.concatenate([line, line[LANES:]], axis=0).T
            ptot[n] = line[0:1]
            if n == 0:
                acc[0, :ROWS, :] = mixed[rows]
                continue
            for p in range(2):
                part[n, p * ROWS : (p + 1) * ROWS, :] = mixed[
                    rows, p * LANES : (p + 1) * LANES
                ].astype(jnp.bfloat16)
            t = (RING - OFFSETS[i]) % RING
            r_copies[t, k].start()
            p_copies[t, k].start()

    image = acc[0, :ROWS, :]
    totals = ptot[0]
    for t in (0, 1, 3, 2):
        for k in range(2):
            if (t, k) == (0, 0):
                continue
            n = target_slot(t, k)
            r_copies[t, k].wait_recv()
            p_copies[t, k].wait_recv()
            image = image + jnp.concatenate([rsb[n, :ROWS, :], rsb[n, ROWS:, :]], axis=1).astype(jnp.float32)
            totals = totals + rst[n]
    dg, rg = dg_ref[...], rg_ref[...]
    dv, rv = dv_ref[...], rv_ref[...]
    image = jnp.sqrt(scale_ref[...]) * image + NUGGET * dg
    image_vals = totals[:, :ROWS] + NUGGET * dv

    def inner(vals, grads):
        first_part = jnp.sum(jnp.sum(grads, axis=0, keepdims=True), axis=1, keepdims=True)
        return first_part + jnp.sum(vals, axis=1, keepdims=True)

    sums = (
        inner(rv * rv, rg * rg),
        inner(dv * image_vals, dg * image),
        inner(rv * image_vals, rg * image),
        inner(image_vals * image_vals, image * image),
    )
    lane_row = lax.broadcasted_iota(jnp.int32, (1, LANES), 1)
    packed = jnp.zeros((1, LANES), jnp.float32)
    for i, value in enumerate(sums):
        packed = jnp.where(lane_row == i, value, packed)
    mine[...] = packed

    me = row * 8 + col

    def spread(i, carry):
        peer = (me + i) % COUNT
        pltpu.make_async_remote_copy(
            src_ref=mine,
            dst_ref=arb.at[me],
            send_sem=a_send,
            recv_sem=a_recv,
            device_id=(peer // 8, peer % 8),
            device_id_type=MESH,
        ).start()
        return carry

    lax.fori_loop(1, COUNT, spread, 0)
    arb[me] = packed
    others = arb.at[pl.ds(0, COUNT - 1)]
    pltpu.make_async_copy(others, others, a_recv).wait()

    every = jnp.sum(arb[...], axis=0)

    def pick(i):
        return jnp.sum(jnp.where(lane_row == i, every, 0.0), axis=1, keepdims=True)

    norm_now, curvature, cross, image_norm = (pick(i) for i in range(4))
    step = norm_now / curvature
    norm_next = norm_now - 2.0 * (step * cross) + step * (step * image_norm)
    ratio = norm_next / norm_now
    next_vals = rv - step * image_vals
    next_grads = rg - step * image
    nsv_ref[...] = sv_ref[...] + step * dv
    nsg_ref[...] = sg_ref[...] + step * dg
    nrv_ref[...] = next_vals
    nrg_ref[...] = next_grads
    ndv_ref[...] = next_vals + ratio * dv
    ndg_ref[...] = next_grads + ratio * dg

    for copy in copies.values():
        copy.wait_send()
    for group in (x_copies, r_copies, p_copies):
        for copy in group.values():
            copy.wait_send()
    pltpu.make_async_copy(others, others, a_send).wait()


def body(points, lengthscale, sv, sg, rv, rg, dv, dg):
    vmem = pl.BlockSpec(memory_space=pltpu.VMEM)
    line = jax.ShapeDtypeStruct((1, ROWS), jnp.float32)
    block = jax.ShapeDtypeStruct((ROWS, DIM), jnp.float32)
    dma = pltpu.SemaphoreType.DMA
    outs = pl.pallas_call(
        kernel,
        out_shape=(line, block) * 3,
        in_specs=[vmem] * 8,
        out_specs=(vmem,) * 6,
        scratch_shapes=[
            pltpu.VMEM((16, BLOCK, LANES), jnp.bfloat16),
            pltpu.VMEM((8, X_ROWS, LANES), jnp.bfloat16),
            pltpu.VMEM((4, 2 * ROWS, LANES), jnp.float32),
            pltpu.VMEM((4, 2 * ROWS, DIM), jnp.float32),
            pltpu.VMEM((4, 2 * ROWS, LANES), jnp.float32),
            pltpu.VMEM((8, X_ROWS, LANES), jnp.bfloat16),
            pltpu.VMEM((8, 1, 2 * LANES), jnp.float32),
            pltpu.VMEM((8, X_ROWS, LANES), jnp.bfloat16),
            pltpu.VMEM((8, 1, 2 * LANES), jnp.float32),
            pltpu.VMEM((V_ROWS, LANES), jnp.float32),
            pltpu.VMEM((1, LANES), jnp.float32),
            pltpu.VMEM((COUNT, 1, LANES), jnp.float32),
            dma((20,)),
            dma((20,)),
            dma((8,)),
            dma((8,)),
            dma((8,)),
            dma((8,)),
            dma((8,)),
            dma((8,)),
            dma,
            dma,
        ],
        compiler_params=pltpu.CompilerParams(
            collective_id=0, has_side_effects=True, vmem_limit_bytes=48 << 20
        ),
        cost_estimate=pl.CostEstimate(
            flops=9_700_000_000, bytes_accessed=2_000_000, transcendentals=4_800_000
        ),
    )(
        points,
        lengthscale.reshape(1, DIM),
        sv.reshape(1, ROWS),
        sg,
        rv.reshape(1, ROWS),
        rg,
        dv.reshape(1, ROWS),
        dg,
    )
    nsv, nsg, nrv, nrg, ndv, ndg = outs
    return (nsv.reshape(ROWS), nsg, nrv.reshape(ROWS), nrg, ndv.reshape(ROWS), ndg)


def solution(mesh):
    lines, blocks = P(("row", "col")), P(("row", "col"), None)
    return jax.shard_map(
        body,
        mesh=mesh,
        in_specs=(blocks, P(), lines, blocks, lines, blocks, lines, blocks),
        out_specs=(lines, blocks) * 3,
        check_vma=False,
    )
```

time: 323 us -> 57.4 us (0.18)
  blocking collectives: 235 us -> 0 us
  Pallas kernels: 0 us -> 48.4 us
  matrix products: 36 us -> 0 us
  between operations: 22 us -> 0.68 us
  other arithmetic: 13.8 us -> 0 us
  waiting for transfers between devices: 9.42 us -> 0 us
    psum x2 -> x0, blocking collectives: 130 us -> none  [the longest x1 67.1 us: body(): lax.psum(squared_norm(residual_vals, residual_grads), ('row', 'col'))]
    unnamed x2 -> x0, blocking collectives: 74.4 us -> none
    pallas_call x0 -> x1, Pallas kernels: none -> 48.4 us  [body(): pl.pallas_call(kernel, out_shape=(line, block) * 3, in_specs=[vmem] * 8,...]
    dot_general x12 -> x0, matrix products: 36 us -> none  [the longest x6 20.9 us: contract(): lax.dot_general(left, right, (((1,), (1,)), ((), ())), preferred_element_...]
    all_gather x2 -> x0, blocking collectives: 29.9 us -> none  [the longest x1 16.4 us: body(): lax.all_gather(scaled, 'col', axis=0, tiled=True)]
    reduce_sum x10 -> x0, other arithmetic: 10.1 us -> none  [the longest x3 3.75 us: one_block(): target_square = jnp.sum(jnp.square(target_tile.astype(jnp.float32)), axis=1)]
    reduce_scatter x1 -> x0, waiting for transfers between devices: 8.35 us -> none  [body(): lax.psum_scatter(mixed_terms, 'row', scatter_dimension=0, tiled=True)]
    unnamed x24 -> x22, local copies, waits for them, and re-layouts: 2.69 us -> 8.08 us
  transfers between devices with their start and end apart: 2 -> 0, of which waited for: 2 -> 0; matrix products, arithmetic and copies ran while one was open for 2% -> 0% of each run, Pallas kernels for 0% -> 0%
where the time goes in v1:
time: 57.4 us; the launch traced here: 57.2 us
  Pallas kernels  48.4 us (84%)
  local copies, waits for them, and re-layouts  8.08 us (14%)
  between operations  0.68 us (1%)
    pallas_call x1, Pallas kernels, body(): pl.pallas_call(kernel, out_shape=(line, block) * 3, in_specs=[vmem] * 8,...  48.4 us
    unnamed x22, local copies, waits for them, and re-layouts  8.08 us

profile of v1, /device:TPU:1, one launch (start us, length us, event | category | flops | bytes accessed | tf_op | source)
XLA Modules:
  0.0 57.2 jit_solution(3072692344570844958)
XLA Ops:
  0.6 0.0 copy-start.7
  0.6 0.0 copy-start.5
  0.7 0.0 copy-start.6
  0.7 0.0 copy-start.4
  0.7 0.6 %copy-done.7 = f32[192]{0:T(256)S(1)} copy-done((f32[192]{0:T(256)S(1)}, f32[192]{0:T(256)}, u32[]{:S(2)}) %copy-start.7) | copy-done | bytes 792
  1.3 0.0 copy-done.5
  1.3 0.0 copy-done.6
  1.3 0.0 copy-done.4
  1.4 0.0 copy-start
  1.4 0.9 %copy-done = f32[192,256]{1,0:T(8,128)S(1)} copy-done((f32[192,256]{1,0:T(8,128)S(1)}, f32[192,256]{1,0:T(8,128)}, u32[]{:S(2)}) %copy-start) | copy-done | bytes 196632
  2.3 0.0 copy-start.1
  2.3 0.9 %copy-done.1 = f32[192,256]{1,0:T(8,128)S(1)} copy-done((f32[192,256]{1,0:T(8,128)S(1)}, f32[192,256]{1,0:T(8,128)}, u32[]{:S(2)}) %copy-start.1) | copy-done | bytes 196632
  3.2 0.0 copy-start.2
  3.2 0.9 %copy-done.2 = f32[192,256]{1,0:T(8,128)S(1)} copy-done((f32[192,256]{1,0:T(8,128)S(1)}, f32[192,256]{1,0:T(8,128)}, u32[]{:S(2)}) %copy-start.2) | copy-done | bytes 196632
  4.1 0.0 copy-start.3
  4.1 0.9 %copy-done.3 = bf16[192,256]{1,0:T(8,128)(2,1)S(1)} copy-done((bf16[192,256]{1,0:T(8,128)(2,1)S(1)}, bf16[192,256]{1,0:T(8,128)(2,1)}, u32[]{:S(2)}) %copy-start.3) | copy-done | bytes 98328
  5.0 48.4 %shard_map.127 = (f32[1,192]{1,0:T(1,128)S(1)}, f32[192,256]{1,0:T(8,128)S(1)}, f32[1,192]{1,0:T(1,128)S(1)}, f32[192,256]{1,0:T(8,128)S(1)}, f32[1,192]{1,0:T(1,128)S(1)}, /*index=5*/f32[192,256]{1,0:T(8,128)S(1)}) custom-call(bf16[192,256]{1,0:T(8,128)(2,1)S(1)} %copy-done.3, f32[1,256]{1,0:T(1,128)S(1)} %bitcast.10, f32[1,192]{1,0:T(1,128)S(1)} %bitcast.11, ...), custom_call_target="tpu_custom_call" | custom-call | flops 9699999744 | bytes 2000000 | tf_op jit(solution)/shard_map/pallas_call | solution.py:415
  53.5 0.6 copy.20
  54.0 0.7 %copy.21 = f32[192,256]{1,0:T(8,128)} copy(f32[192,256]{1,0:T(8,128)S(1)} %get-tuple-element.25) | data formatting | bytes 393216
  54.7 0.6 copy.22
  55.3 0.7 %copy.23 = f32[192,256]{1,0:T(8,128)} copy(f32[192,256]{1,0:T(8,128)S(1)} %get-tuple-element.27) | data formatting | bytes 393216
  56.0 0.6 copy.24
  56.5 0.7 %copy.25 = f32[192,256]{1,0:T(8,128)} copy(f32[192,256]{1,0:T(8,128)S(1)} %get-tuple-element.29) | data formatting | bytes 393216
Async XLA Ops:
  0.6 0.7 %copy-start.7 = (f32[192]{0:T(256)S(1)}, f32[192]{0:T(256)}, u32[]{:S(2)}) copy-start(f32[192]{0:T(256)} %param.14) | copy-start | bytes 2308
  0.6 0.7 %copy-start.5 = (f32[192]{0:T(256)S(1)}, f32[192]{0:T(256)}, u32[]{:S(2)}) copy-start(f32[192]{0:T(256)} %param.10) | copy-start | bytes 2308
  0.7 0.7 %copy-start.6 = (f32[192]{0:T(256)S(1)}, f32[192]{0:T(256)}, u32[]{:S(2)}) copy-start(f32[192]{0:T(256)} %param.12) | copy-start | bytes 2308
  0.7 0.7 %copy-start.4 = (f32[256]{0:T(256)S(1)}, f32[256]{0:T(256)}, u32[]{:S(2)}) copy-start(f32[256]{0:T(256)} %param.9) | copy-start | bytes 3076
  1.4 0.9 %copy-start = (f32[192,256]{1,0:T(8,128)S(1)}, f32[192,256]{1,0:T(8,128)}, u32[]{:S(2)}) copy-start(f32[192,256]{1,0:T(8,128)} %sg_ref.1) | copy-start | bytes 589828
  2.3 0.9 %copy-start.1 = (f32[192,256]{1,0:T(8,128)S(1)}, f32[192,256]{1,0:T(8,128)}, u32[]{:S(2)}) copy-start(f32[192,256]{1,0:T(8,128)} %rg_ref.1) | copy-start | bytes 589828
  3.2 0.9 %copy-start.2 = (f32[192,256]{1,0:T(8,128)S(1)}, f32[192,256]{1,0:T(8,128)}, u32[]{:S(2)}) copy-start(f32[192,256]{1,0:T(8,128)} %dg_ref.1) | copy-start | bytes 589828
  4.1 0.9 %copy-start.3 = (bf16[192,256]{1,0:T(8,128)(2,1)S(1)}, bf16[192,256]{1,0:T(8,128)(2,1)}, u32[]{:S(2)}) copy-start(bf16[192,256]{1,0:T(8,128)(2,1)} %points_ref.1) | copy-start | bytes 294916

commit v2 on v1

--- a/solution.py
+++ b/solution.py
@@ -17,17 +17,24 @@
 LANES = 128
 TAIL = ROWS - LANES
 X_ROWS = 2 * ROWS
-S_ROWS = 2 * ROWS
-V_ROWS = 16
-BLOCK = X_ROWS + S_ROWS + V_ROWS
-CUT = X_ROWS
+PLANES = (0, ROWS, 2 * ROWS, 3 * ROWS + 16)
+VECTORS = slice(3 * ROWS, 3 * ROWS + 16)
+BLOCK = 4 * ROWS + 16
+SPLIT = PLANES[3]
+CUT = 288
 OFFSETS = (0, 1, 3, 2)
 COUNT = 128
+GRANT = 62 << 20
+ORDER = (
+    ((0, 0), (1, 0), (3, 0), (0, 1))
+    + ((0, 3), (2, 0), (0, 2), (1, 1))
+    + ((1, 3), (3, 1), (3, 3), (2, 1))
+    + ((2, 3), (1, 2), (3, 2), (2, 2))
+)
 
 
 def slot_of(f, s):
-    fi, si = OFFSETS.index(f % RING), OFFSETS.index(s % RING)
-    return fi if si == 0 else 4 + 3 * fi + si - 1
+    return ORDER.index((f, s))
 
 
 def target_slot(t, k):
@@ -35,20 +42,23 @@
 
 
 def kernel(
+    points_hbm,
+    scale_hbm,
+    rv_hbm,
+    rg_hbm,
+    dv_hbm,
+    dg_hbm,
+    vals_hbm,
+    image_hbm,
+    steps_hbm,
+    vals_ref,
+    image_ref,
     points_ref,
     scale_ref,
-    sv_ref,
-    sg_ref,
     rv_ref,
     rg_ref,
     dv_ref,
     dg_ref,
-    nsv_ref,
-    nsg_ref,
-    nrv_ref,
-    nrg_ref,
-    ndv_ref,
-    ndg_ref,
     slots,
     tx,
     ta,
@@ -71,6 +81,7 @@
     p_recv,
     a_send,
     a_recv,
+    loads,
 ):
     row, col = lax.axis_index("row"), lax.axis_index("col")
     z, y = row // RING, row % RING
@@ -93,13 +104,27 @@
     for peer in near:
         pl.semaphore_signal(barrier, inc=1, device_id=peer, device_id_type=MESH)
 
+    pairs = (
+        (points_hbm, points_ref),
+        (scale_hbm, scale_ref),
+        (dg_hbm, dg_ref),
+        (dv_hbm, dv_ref),
+        (rg_hbm, rg_ref),
+        (rv_hbm, rv_ref),
+    )
+    arrivals = [pltpu.make_async_copy(a, b, loads.at[i]) for i, (a, b) in enumerate(pairs)]
+    for arrival in arrivals:
+        arrival.start()
+    for arrival in arrivals[:4]:
+        arrival.wait()
+
     root = jnp.sqrt(scale_ref[...])
     scaled = (points_ref[...].astype(jnp.float32) * root).astype(jnp.bfloat16)
     slope = (dg_ref[...] * root).astype(jnp.bfloat16)
     for p in range(2):
         lanes = slice(p * LANES, (p + 1) * LANES)
         slots[0, p * ROWS : (p + 1) * ROWS, :] = scaled[:, lanes]
-        slots[0, X_ROWS + p * ROWS : X_ROWS + (p + 1) * ROWS, :] = slope[:, lanes]
+        slots[0, PLANES[2 + p] : PLANES[2 + p] + ROWS, :] = slope[:, lanes]
         tx[0, p * ROWS : (p + 1) * ROWS, :] = scaled[:, lanes]
     wide = scaled.astype(jnp.float32)
     square = jnp.sum(wide * wide, axis=1, keepdims=True)
@@ -122,32 +147,50 @@
             piece = term.astype(jnp.bfloat16).astype(jnp.float32)
             vecs[3 * i + j : 3 * i + j + 1, :] = piece
             term = term - piece
-    slots[0, X_ROWS + S_ROWS :, :] = vecs[...].astype(jnp.bfloat16)
-
-    copies = {}
-
-    def describe(f, s, half, source, peer):
-        n = len(copies)
-        where = {None: slice(0, BLOCK), 0: slice(0, CUT), 1: slice(CUT, BLOCK)}[half]
-        rows = pl.ds(where.start, where.stop - where.start)
-        copies[f, s, half] = pltpu.make_async_remote_copy(
-            src_ref=slots.at[slot_of(*source), rows],
-            dst_ref=slots.at[slot_of(f, s), rows],
+    slots[0, VECTORS, :] = vecs[...].astype(jnp.bfloat16)
+
+    upper, lower = {}, {}
+
+    def describe(group, key, slot, source, top, stop, peer):
+        n = len(upper) + len(lower)
+        group[key] = pltpu.make_async_remote_copy(
+            src_ref=slots.at[source, pl.ds(top, stop - top)],
+            dst_ref=slots.at[slot, pl.ds(top, stop - top)],
             send_sem=g_send.at[n],
             recv_sem=g_recv.at[n],
             device_id=peer,
             device_id_type=MESH,
         )
 
-    describe(1, 0, None, (0, 0), first(3))
-    describe(3, 0, None, (0, 0), first(1))
-    describe(2, 0, 0, (3, 0), first(1))
-    describe(2, 0, 1, (1, 0), first(3))
+    def whole(f, s, source, peer):
+        describe(upper, (f, s), slot_of(f, s), slot_of(*source), 0, SPLIT, peer)
+
+    def halves(f, s, behind, ahead, forward, back):
+        describe(upper, (f, s, 0), slot_of(f, s), slot_of(*behind), 0, CUT, forward)
+        describe(upper, (f, s, 1), slot_of(f, s), slot_of(*ahead), CUT, SPLIT, back)
+
+    whole(1, 0, (0, 0), first(3))
+    whole(3, 0, (0, 0), first(1))
+    halves(2, 0, (3, 0), (1, 0), first(1), first(3))
     for f in OFFSETS:
-        describe(f, 1, None, (f, 0), second(3, c))
-        describe(f, 3, None, (f, 0), second(1, c))
-        describe(f, 2, 0, (f, 3), second(1, c))
-        describe(f, 2, 1, (f, 1), second(3, c))
+        whole(f, 1, (f, 0), second(3, c))
+        whole(f, 3, (f, 0), second(1, c))
+        halves(f, 2, (f, 3), (f, 1), second(1, c), second(3, c))
+
+    def other(f, s, source, peer):
+        describe(lower, (f, s), slot_of(f, s), source, SPLIT, BLOCK, peer)
+
+    def across_core(behind, ahead):
+        return slot_of(*behind) * o + slot_of(*ahead) * c
+
+    away = 1 + 2 * c
+    other(0, 1, slot_of(0, 0), second(3, c))
+    other(0, 3, slot_of(0, 0), second(1, c))
+    other(0, 2, across_core((0, 3), (0, 1)), second(away, c))
+    for s in OFFSETS:
+        other(1, s, slot_of(0, s), first(3))
+        other(3, s, slot_of(0, s), first(1))
+        other(2, s, across_core((3, s), (1, s)), first(away))
 
     x_copies, r_copies, p_copies = {}, {}, {}
     for t in OFFSETS:
@@ -196,28 +239,25 @@
 
     low = lax.broadcasted_iota(jnp.int32, (1, LANES), 1) < TAIL
 
-    def sources(g):
-        held = range(4 * g, 4 * g + 4)
-
+    def sources(heads, tails):
         def plane(p):
-            top = p * ROWS
-            pieces = [slots[s, top : top + LANES, :] for s in held]
-            pieces += [slots[s, top + LANES : top + ROWS, :] for s in held]
+            top = PLANES[p]
+            pieces = [slots[s, top : top + LANES, :] for s in heads]
+            pieces += [slots[s, top + LANES : top + ROWS, :] for s in tails]
             return jnp.concatenate(pieces, axis=0)
 
         xs = jnp.concatenate([plane(0), plane(1)], axis=1)
         ss = jnp.concatenate([plane(2), plane(3)], axis=1)
 
         def vector(i):
-            heads, tails = [], []
-            for s in held:
-                v = slots[s, X_ROWS + S_ROWS :, :].astype(jnp.float32)
-                heads.append(v[3 * i : 3 * i + 1] + v[3 * i + 1 : 3 * i + 2] + v[3 * i + 2 : 3 * i + 3])
-                j = 3 * i + 3
-                tails.append(v[j : j + 1] + v[j + 1 : j + 2] + v[j + 2 : j + 3])
-            heads.append(jnp.where(low, tails[0], tails[1]))
-            heads.append(jnp.where(low, tails[2], tails[3]))
-            return jnp.concatenate(heads, axis=1)
+            def read(s, j):
+                v = slots[s, VECTORS, :].astype(jnp.float32)
+                return v[j : j + 1] + v[j + 1 : j + 2] + v[j + 2 : j + 3]
+
+            pieces = [read(s, 3 * i) for s in heads]
+            ends = [read(s, 3 * i + 3) for s in tails]
+            pieces += [jnp.where(low, u, v) for u, v in zip(ends[::2], ends[1::2])]
+            return jnp.concatenate(pieces, axis=1)
 
         return xs, ss, vector(0), vector(2)
 
@@ -226,91 +266,97 @@
             left, right, (((1,), (1,)), ((), ())), preferred_element_type=jnp.float32
         )
 
-    def tile_terms(g, loaded, i):
+    def tile_terms(loaded, i, fresh=False):
         xs, ss, sb, sc = loaded
         points = tile_points(i)
-        base = jnp.concatenate([ta[i]] * 6, axis=1)
+        wide = xs.shape[0] // LANES
+        base = jnp.concatenate([ta[i]] * wide, axis=1)
         kern = jnp.exp2(contract(points, xs) * LOG2E + (base + sb))
         weight = kern * (contract(points, ss) + sc)
         total = weight[:, :LANES]
-        for q in range(1, 6):
+        for q in range(1, wide):
             total = total + weight[:, q * LANES : (q + 1) * LANES]
         pair = jnp.concatenate([kern.astype(jnp.bfloat16), weight.astype(jnp.bfloat16)], axis=1)
         mixed = jnp.dot(
             pair, jnp.concatenate([ss, xs], axis=0), preferred_element_type=jnp.float32
         )
-        if g > 0:
+        if not fresh:
             mixed, total = mixed + acc[i], total + tot[i]
         return mixed, total
 
     def compute(g, tiles):
-        loaded = sources(g)
+        held = range(4 * g, 4 * g + 4)
+        loaded = sources(held, held)
         for i in tiles:
-            mixed, total = tile_terms(g, loaded, i)
+            mixed, total = tile_terms(loaded, i, fresh=g == 0)
             acc[i] = mixed
             tot[i] = total
 
+    def start(*some):
+        for copy in some:
+            copy.start()
+
+    def landed(*some):
+        for copy in some:
+            copy.wait_recv()
+
     pl.semaphore_wait(barrier, len(near))
-    copies[1, 0, None].start()
-    copies[3, 0, None].start()
-    x_copies[0, 1].start()
+    start(upper[1, 0], upper[3, 0], lower[0, 1], lower[0, 3])
+    start(x_copies[0, 1])
     for t in (2, 1, 3):
-        x_copies[t, 0].start()
-        x_copies[t, 1].start()
-    copies[0, 1, None].start()
-    copies[0, 3, None].start()
-
-    copies[3, 0, None].wait_recv()
-    copies[2, 0, 0].start()
-    copies[1, 0, None].wait_recv()
-    copies[2, 0, 1].start()
-    for f in (1, 3):
-        copies[f, 1, None].start()
-        copies[f, 3, None].start()
-
-    def relay(f):
-        copies[f, 3, None].wait_recv()
-        copies[f, 2, 0].start()
-        copies[f, 1, None].wait_recv()
-        copies[f, 2, 1].start()
-
-    def settle(f):
-        copies[f, 2, 0].wait_recv()
-        copies[f, 2, 1].wait_recv()
-
-    x_copies[0, 1].wait_recv()
+        start(x_copies[t, 0], x_copies[t, 1])
+    start(upper[0, 1], upper[0, 3], lower[1, 0], lower[3, 0])
+
+    landed(lower[0, 1], lower[0, 3])
+    start(lower[0, 2])
+    start(*(lower[f, s] for s in (1, 3) for f in (1, 3)))
+    landed(upper[3, 0], upper[1, 0])
+    start(upper[2, 0, 0], upper[2, 0, 1])
+    start(*(upper[f, s] for f in (1, 3) for s in (1, 3)))
+
+    landed(x_copies[0, 1])
     target_base(0)
     for i, t in ((1, 1), (2, 3)):
-        x_copies[t, 0].wait_recv()
-        x_copies[t, 1].wait_recv()
+        landed(x_copies[t, 0], x_copies[t, 1])
         target_base(i)
-    settle_first = (copies[2, 0, 0], copies[2, 0, 1])
-    for copy in settle_first:
-        copy.wait_recv()
-    copies[2, 1, None].start()
-    copies[2, 3, None].start()
-
+    landed(upper[0, 3], upper[0, 1])
+    start(upper[0, 2, 0], upper[0, 2, 1])
+    landed(lower[1, 0], lower[3, 0])
+    start(lower[2, 0])
     compute(0, (0, 1))
-    relay(0)
-    x_copies[2, 0].wait_recv()
-    x_copies[2, 1].wait_recv()
+
+    landed(x_copies[2, 0], x_copies[2, 1])
     target_base(3)
+    landed(lower[0, 2])
+    start(lower[1, 2], lower[3, 2])
+    landed(upper[2, 0, 0], upper[2, 0, 1])
+    start(upper[2, 1], upper[2, 3])
     compute(0, (2, 3))
-    relay(1)
-    settle(0)
+
+    landed(lower[1, 1], lower[3, 1], lower[1, 3], lower[3, 3])
+    start(lower[2, 1], lower[2, 3])
+    landed(upper[1, 1], upper[1, 3])
+    start(upper[1, 2, 0], upper[1, 2, 1])
+    landed(upper[3, 1], upper[3, 3])
+    start(upper[3, 2, 0], upper[3, 2, 1])
+    landed(upper[0, 2, 0], upper[0, 2, 1], lower[2, 0])
     compute(1, (0, 1))
-    relay(3)
+    landed(lower[1, 2], lower[3, 2])
+    start(lower[2, 2])
     compute(1, (2, 3))
-    settle(1)
-    compute(2, (0, 1))
-    relay(2)
-    compute(2, (2, 3))
-    settle(3)
-    settle(2)
-
-    loaded = sources(3)
+    landed(upper[2, 1], upper[2, 3])
+    start(upper[2, 2, 0], upper[2, 2, 1])
+    landed(lower[2, 1])
+    compute(2, (0, 1, 2, 3))
+    landed(lower[2, 3], upper[1, 2, 0], upper[1, 2, 1], upper[3, 2, 0], upper[3, 2, 1])
+    loaded = sources((12, 13, 14), (12, 13))
+    for i in range(4):
+        acc[i], tot[i] = tile_terms(loaded, i)
+    landed(lower[2, 2], upper[2, 2, 0], upper[2, 2, 1])
+
+    loaded = sources((15,), (14, 15))
     for i in (3, 1, 2, 0):
-        mixed, total = tile_terms(3, loaded, i)
+        mixed, total = tile_terms(loaded, i)
         total = jnp.sum(total, axis=1, keepdims=True)
         mixed = mixed - tile_points(i).astype(jnp.float32) * total
         for k in range(2):
@@ -341,10 +387,21 @@
             p_copies[t, k].wait_recv()
             image = image + jnp.concatenate([rsb[n, :ROWS, :], rsb[n, ROWS:, :]], axis=1).astype(jnp.float32)
             totals = totals + rst[n]
+    for arrival in arrivals[4:]:
+        arrival.wait()
     dg, rg = dg_ref[...], rg_ref[...]
     dv, rv = dv_ref[...], rv_ref[...]
     image = jnp.sqrt(scale_ref[...]) * image + NUGGET * dg
     image_vals = totals[:, :ROWS] + NUGGET * dv
+
+    vals_ref[...] = image_vals
+    image_ref[...] = image
+    stores = [
+        pltpu.make_async_copy(vals_ref, vals_hbm, loads.at[1]),
+        pltpu.make_async_copy(image_ref, image_hbm, loads.at[2]),
+    ]
+    for store in stores:
+        store.start()
 
     def inner(vals, grads):
         first_part = jnp.sum(jnp.sum(grads, axis=0, keepdims=True), axis=1, keepdims=True)
@@ -390,34 +447,60 @@
     step = norm_now / curvature
     norm_next = norm_now - 2.0 * (step * cross) + step * (step * image_norm)
     ratio = norm_next / norm_now
-    next_vals = rv - step * image_vals
-    next_grads = rg - step * image
-    nsv_ref[...] = sv_ref[...] + step * dv
-    nsg_ref[...] = sg_ref[...] + step * dg
-    nrv_ref[...] = next_vals
-    nrg_ref[...] = next_grads
-    ndv_ref[...] = next_vals + ratio * dv
-    ndg_ref[...] = next_grads + ratio * dg
-
-    for copy in copies.values():
-        copy.wait_send()
-    for group in (x_copies, r_copies, p_copies):
+    pltpu.make_async_copy(others, others, a_send).wait()
+    mine[...] = jnp.where(lane_row == 0, step, ratio)
+    last = pltpu.make_async_copy(mine, steps_hbm, loads.at[0])
+    last.start()
+
+    for group in (upper, lower, x_copies, r_copies, p_copies):
         for copy in group.values():
             copy.wait_send()
-    pltpu.make_async_copy(others, others, a_send).wait()
+    for store in stores:
+        store.wait()
+    last.wait()
+
+
+def update(*refs):
+    sources, results, held = refs[:9], refs[9:15], refs[15:29]
+    steps, arrived, left = refs[29:]
+    landing = held[:8] + (steps,)
+    loads = [pltpu.make_async_copy(a, b, arrived.at[i]) for i, (a, b) in enumerate(zip(sources, landing))]
+    for load in loads:
+        load.start()
+    for load in loads:
+        load.wait()
+    sv, sg, rv, rg, dv, dg, iv, ig = (ref[...] for ref in landing[:8])
+    step, ratio = steps[:, 0:1], steps[:, 1:2]
+    nrv, nrg = rv - step * iv, rg - step * ig
+    values = (sv + step * dv, sg + step * dg, nrv, nrg, nrv + ratio * dv, nrg + ratio * dg)
+    stores = []
+    for i, value in enumerate(values):
+        held[8 + i][...] = value
+        stores.append(pltpu.make_async_copy(held[8 + i], results[i], left.at[i]))
+        stores[i].start()
+    for store in stores:
+        store.wait()
 
 
 def body(points, lengthscale, sv, sg, rv, rg, dv, dg):
-    vmem = pl.BlockSpec(memory_space=pltpu.VMEM)
+    hbm = pl.BlockSpec(memory_space=pltpu.HBM)
     line = jax.ShapeDtypeStruct((1, ROWS), jnp.float32)
     block = jax.ShapeDtypeStruct((ROWS, DIM), jnp.float32)
     dma = pltpu.SemaphoreType.DMA
-    outs = pl.pallas_call(
+    image_vals, image_grads, steps = pl.pallas_call(
         kernel,
-        out_shape=(line, block) * 3,
-        in_specs=[vmem] * 8,
-        out_specs=(vmem,) * 6,
+        out_shape=(line, block, jax.ShapeDtypeStruct((1, LANES), jnp.float32)),
+        in_specs=[hbm] * 6,
+        out_specs=(hbm,) * 3,
         scratch_shapes=[
+            pltpu.VMEM((1, ROWS), jnp.float32),
+            pltpu.VMEM((ROWS, DIM), jnp.float32),
+            pltpu.VMEM((ROWS, DIM), jnp.bfloat16),
+            pltpu.VMEM((1, DIM), jnp.float32),
+            pltpu.VMEM((1, ROWS), jnp.float32),
+            pltpu.VMEM((ROWS, DIM), jnp.float32),
+            pltpu.VMEM((1, ROWS), jnp.float32),
+            pltpu.VMEM((ROWS, DIM), jnp.float32),
             pltpu.VMEM((16, BLOCK, LANES), jnp.bfloat16),
             pltpu.VMEM((8, X_ROWS, LANES), jnp.bfloat16),
             pltpu.VMEM((4, 2 * ROWS, LANES), jnp.float32),
@@ -427,11 +510,11 @@
             pltpu.VMEM((8, 1, 2 * LANES), jnp.float32),
             pltpu.VMEM((8, X_ROWS, LANES), jnp.bfloat16),
             pltpu.VMEM((8, 1, 2 * LANES), jnp.float32),
-            pltpu.VMEM((V_ROWS, LANES), jnp.float32),
+            pltpu.VMEM((16, LANES), jnp.float32),
             pltpu.VMEM((1, LANES), jnp.float32),
             pltpu.VMEM((COUNT, 1, LANES), jnp.float32),
-            dma((20,)),
-            dma((20,)),
+            dma((35,)),
+            dma((35,)),
             dma((8,)),
             dma((8,)),
             dma((8,)),
@@ -440,9 +523,10 @@
             dma((8,)),
             dma,
             dma,
+            dma((6,)),
         ],
         compiler_params=pltpu.CompilerParams(
-            collective_id=0, has_side_effects=True, vmem_limit_bytes=48 << 20
+            collective_id=0, has_side_effects=True, vmem_limit_bytes=GRANT
         ),
         cost_estimate=pl.CostEstimate(
             flops=9_700_000_000, bytes_accessed=2_000_000, transcendentals=4_800_000
@@ -450,14 +534,30 @@
     )(
         points,
         lengthscale.reshape(1, DIM),
+        rv.reshape(1, ROWS),
+        rg,
+        dv.reshape(1, ROWS),
+        dg,
+    )
+    nsv, nsg, nrv, nrg, ndv, ndg = pl.pallas_call(
+        update,
+        out_shape=(line, block) * 3,
+        in_specs=[hbm] * 9,
+        out_specs=(hbm,) * 6,
+        scratch_shapes=[pltpu.VMEM((1, ROWS), jnp.float32), pltpu.VMEM((ROWS, DIM), jnp.float32)] * 7
+        + [pltpu.VMEM((1, LANES), jnp.float32), dma((9,)), dma((6,))],
+        compiler_params=pltpu.CompilerParams(vmem_limit_bytes=GRANT),
+    )(
         sv.reshape(1, ROWS),
         sg,
         rv.reshape(1, ROWS),
         rg,
         dv.reshape(1, ROWS),
         dg,
+        image_vals,
+        image_grads,
+        steps,
     )
-    nsv, nsg, nrv, nrg, ndv, ndg = outs
     return (nsv.reshape(ROWS), nsg, nrv.reshape(ROWS), nrg, ndv.reshape(ROWS), ndg)
 
 

time: 57.4 us -> 47.7 us (0.83)
  local copies, waits for them, and re-layouts: 8.08 us -> 0 us
  Pallas kernels: 48.4 us -> 46.9 us
    unnamed x22 -> x0, local copies, waits for them, and re-layouts: 8.08 us -> none
    pallas_call x1 -> x2, Pallas kernels: 48.4 us -> 46.9 us  [the longest x1 44.6 us: body(): pl.pallas_call(kernel, out_shape=(line, block, jax.ShapeDtypeStruct((1, L...]
where the time goes in v2:
time: 47.7 us; the launch traced here: 47.5 us
  Pallas kernels  46.9 us (98%)
  between operations  0.64 us (1%)
    pallas_call x1, Pallas kernels, body(): pl.pallas_call(kernel, out_shape=(line, block, jax.ShapeDtypeStruct((1, L...  44.6 us
    pallas_call x1, Pallas kernels, body(): pl.pallas_call(update, out_shape=(line, block) * 3, in_specs=[hbm] * 9, o...  2.33 us

profile of v2, /device:TPU:1, one launch (start us, length us, event | category | flops | bytes accessed | tf_op | source)
XLA Modules:
  0.0 47.5 jit_solution(7484776405259383410)
XLA Ops:
  0.6 44.6 %shard_map.127 = (f32[1,192]{1,0:T(1,128)}, f32[192,256]{1,0:T(8,128)}, f32[1,128]{1,0:T(1,128)}) custom-call(bf16[192,256]{1,0:T(8,128)(2,1)} %points_hbm.1, f32[1,256]{1,0:T(1,128)} %bitcast.12, f32[1,192]{1,0:T(1,128)} %bitcast.8, f32[192,256]{1,0:T(8,128)} %refs_3_.1, f32[1,192]{1,0:T(1,128)} %bitcast.10, f32[192,256]{1,0:T(8,128)} %refs_5_.1), custom_call_target="tpu_custom_call" | custom-call | flops 9699999744 | bytes 2000000 | tf_op jit(solution)/shard_map/pallas_call | solution.py:490
  45.2 2.3 %shard_map.128 = (f32[1,192]{1,0:T(1,128)}, f32[192,256]{1,0:T(8,128)}, f32[1,192]{1,0:T(1,128)}, f32[192,256]{1,0:T(8,128)}, f32[1,192]{1,0:T(1,128)}, /*index=5*/f32[192,256]{1,0:T(8,128)}) custom-call(f32[1,192]{1,0:T(1,128)} %bitcast.7, f32[192,256]{1,0:T(8,128)} %refs_1_.1, f32[1,192]{1,0:T(1,128)} %bitcast.9, f32[192,256]{1,0:T(8,128)} %refs_3_.1, ...), custom_call_target="tpu_custom_call" | custom-call | tf_op jit(solution)/shard_map/pallas_call | solution.py:542

commit v3 on v2

--- a/solution.py
+++ b/solution.py
@@ -26,10 +26,18 @@
 COUNT = 128
 GRANT = 62 << 20
 ORDER = (
-    ((0, 0), (1, 0), (3, 0), (0, 1))
-    + ((0, 3), (2, 0), (0, 2), (1, 1))
-    + ((1, 3), (3, 1), (3, 3), (2, 1))
-    + ((2, 3), (1, 2), (3, 2), (2, 2))
+    ((0, 0), (1, 0), (3, 0))
+    + ((0, 1), (0, 3), (2, 0))
+    + ((1, 1), (1, 3), (3, 1), (3, 3))
+    + ((0, 2), (2, 1), (2, 3))
+    + ((1, 2), (3, 2), (2, 2))
+)
+GROUPS = (
+    ((0, 1, 2), (0, 1)),
+    ((3, 4, 5), (2, 3, 4, 5)),
+    ((6, 7, 8, 9), (6, 7, 8, 9)),
+    ((10, 11, 12), (10, 11)),
+    ((13, 14, 15), (12, 13, 14, 15)),
 )
 
 
@@ -162,6 +170,10 @@
             device_id_type=MESH,
         )
 
+    def pieces(f, s, source, peer):
+        describe(upper, (f, s, 0), slot_of(f, s), slot_of(*source), 0, CUT, peer)
+        describe(upper, (f, s, 1), slot_of(f, s), slot_of(*source), CUT, SPLIT, peer)
+
     def whole(f, s, source, peer):
         describe(upper, (f, s), slot_of(f, s), slot_of(*source), 0, SPLIT, peer)
 
@@ -169,12 +181,13 @@
         describe(upper, (f, s, 0), slot_of(f, s), slot_of(*behind), 0, CUT, forward)
         describe(upper, (f, s, 1), slot_of(f, s), slot_of(*ahead), CUT, SPLIT, back)
 
-    whole(1, 0, (0, 0), first(3))
-    whole(3, 0, (0, 0), first(1))
+    pieces(1, 0, (0, 0), first(3))
+    pieces(3, 0, (0, 0), first(1))
     halves(2, 0, (3, 0), (1, 0), first(1), first(3))
     for f in OFFSETS:
-        whole(f, 1, (f, 0), second(3, c))
-        whole(f, 3, (f, 0), second(1, c))
+        cast = pieces if f == 2 else whole
+        cast(f, 1, (f, 0), second(3, c))
+        cast(f, 3, (f, 0), second(1, c))
         halves(f, 2, (f, 3), (f, 1), second(1, c), second(3, c))
 
     def other(f, s, source, peer):
@@ -285,8 +298,7 @@
         return mixed, total
 
     def compute(g, tiles):
-        held = range(4 * g, 4 * g + 4)
-        loaded = sources(held, held)
+        loaded = sources(*GROUPS[g])
         for i in tiles:
             mixed, total = tile_terms(loaded, i, fresh=g == 0)
             acc[i] = mixed
@@ -301,60 +313,71 @@
             copy.wait_recv()
 
     pl.semaphore_wait(barrier, len(near))
-    start(upper[1, 0], upper[3, 0], lower[0, 1], lower[0, 3])
+    start(upper[3, 0, 0], upper[1, 0, 1], lower[0, 1], lower[0, 3])
+    start(upper[3, 0, 1], upper[1, 0, 0])
     start(x_copies[0, 1])
-    for t in (2, 1, 3):
+    for t in (1, 3):
         start(x_copies[t, 0], x_copies[t, 1])
     start(upper[0, 1], upper[0, 3], lower[1, 0], lower[3, 0])
-
+    start(x_copies[2, 0], x_copies[2, 1])
+
+    landed(upper[3, 0, 0])
+    start(upper[2, 0, 0])
+    landed(upper[1, 0, 1])
+    start(upper[2, 0, 1])
     landed(lower[0, 1], lower[0, 3])
     start(lower[0, 2])
     start(*(lower[f, s] for s in (1, 3) for f in (1, 3)))
-    landed(upper[3, 0], upper[1, 0])
-    start(upper[2, 0, 0], upper[2, 0, 1])
+    landed(upper[3, 0, 1], upper[1, 0, 0])
     start(*(upper[f, s] for f in (1, 3) for s in (1, 3)))
-
     landed(x_copies[0, 1])
     target_base(0)
     for i, t in ((1, 1), (2, 3)):
         landed(x_copies[t, 0], x_copies[t, 1])
         target_base(i)
+    landed(lower[1, 0], lower[3, 0])
+    start(lower[2, 0])
+    compute(0, (0, 1, 2))
+
+    landed(upper[2, 0, 0])
+    start(upper[2, 3, 0], upper[2, 1, 0])
+    landed(upper[2, 0, 1])
+    start(upper[2, 1, 1], upper[2, 3, 1])
     landed(upper[0, 3], upper[0, 1])
     start(upper[0, 2, 0], upper[0, 2, 1])
-    landed(lower[1, 0], lower[3, 0])
-    start(lower[2, 0])
-    compute(0, (0, 1))
-
+    landed(lower[0, 2])
+    start(lower[1, 2], lower[3, 2])
     landed(x_copies[2, 0], x_copies[2, 1])
     target_base(3)
-    landed(lower[0, 2])
-    start(lower[1, 2], lower[3, 2])
-    landed(upper[2, 0, 0], upper[2, 0, 1])
-    start(upper[2, 1], upper[2, 3])
-    compute(0, (2, 3))
+    compute(0, (3,))
+    landed(lower[2, 0])
+    compute(1, (0, 1))
 
     landed(lower[1, 1], lower[3, 1], lower[1, 3], lower[3, 3])
     start(lower[2, 1], lower[2, 3])
+    compute(1, (2, 3))
+
     landed(upper[1, 1], upper[1, 3])
     start(upper[1, 2, 0], upper[1, 2, 1])
     landed(upper[3, 1], upper[3, 3])
     start(upper[3, 2, 0], upper[3, 2, 1])
-    landed(upper[0, 2, 0], upper[0, 2, 1], lower[2, 0])
-    compute(1, (0, 1))
+    compute(2, (0, 1))
+
+    landed(upper[2, 3, 0])
+    start(upper[2, 2, 0])
+    landed(upper[2, 1, 1])
+    start(upper[2, 2, 1])
     landed(lower[1, 2], lower[3, 2])
     start(lower[2, 2])
-    compute(1, (2, 3))
-    landed(upper[2, 1], upper[2, 3])
-    start(upper[2, 2, 0], upper[2, 2, 1])
-    landed(lower[2, 1])
-    compute(2, (0, 1, 2, 3))
-    landed(lower[2, 3], upper[1, 2, 0], upper[1, 2, 1], upper[3, 2, 0], upper[3, 2, 1])
-    loaded = sources((12, 13, 14), (12, 13))
-    for i in range(4):
-        acc[i], tot[i] = tile_terms(loaded, i)
-    landed(lower[2, 2], upper[2, 2, 0], upper[2, 2, 1])
-
-    loaded = sources((15,), (14, 15))
+    compute(2, (2, 3))
+
+    landed(upper[0, 2, 0], upper[0, 2, 1], upper[2, 1, 0], upper[2, 3, 1], lower[2, 1], lower[2, 3])
+    compute(3, (0, 1, 2, 3))
+    for f in (1, 3, 2):
+        landed(upper[f, 2, 0], upper[f, 2, 1])
+    landed(lower[2, 2])
+
+    loaded = sources(*GROUPS[4])
     for i in (3, 1, 2, 0):
         mixed, total = tile_terms(loaded, i)
         total = jnp.sum(total, axis=1, keepdims=True)
@@ -513,8 +536,8 @@
             pltpu.VMEM((16, LANES), jnp.float32),
             pltpu.VMEM((1, LANES), jnp.float32),
             pltpu.VMEM((COUNT, 1, LANES), jnp.float32),
-            dma((35,)),
-            dma((35,)),
+            dma((39,)),
+            dma((39,)),
             dma((8,)),
             dma((8,)),
             dma((8,)),

time: 47.7 us -> 46.1 us (0.966)
  Pallas kernels: 46.9 us -> 45.3 us
    pallas_call x1, Pallas kernels: 44.6 us -> 43 us  [body(): pl.pallas_call(kernel, out_shape=(line, block, jax.ShapeDtypeStruct((1, L...]
where the time goes in v3:
time: 46.1 us; the launch traced here: 46 us
  Pallas kernels  45.3 us (98%)
  between operations  0.64 us (1%)
    pallas_call x1, Pallas kernels, body(): pl.pallas_call(kernel, out_shape=(line, block, jax.ShapeDtypeStruct((1, L...  43 us
    pallas_call x1, Pallas kernels, body(): pl.pallas_call(update, out_shape=(line, block) * 3, in_specs=[hbm] * 9, o...  2.33 us

profile of v3, /device:TPU:1, one launch (start us, length us, event | category | flops | bytes accessed | tf_op | source)
XLA Modules:
  0.0 46.0 jit_solution(11179677662204282322)
XLA Ops:
  0.6 43.0 %shard_map.127 = (f32[1,192]{1,0:T(1,128)}, f32[192,256]{1,0:T(8,128)}, f32[1,128]{1,0:T(1,128)}) custom-call(bf16[192,256]{1,0:T(8,128)(2,1)} %points_hbm.1, f32[1,256]{1,0:T(1,128)} %bitcast.12, f32[1,192]{1,0:T(1,128)} %bitcast.8, f32[192,256]{1,0:T(8,128)} %refs_3_.1, f32[1,192]{1,0:T(1,128)} %bitcast.10, f32[192,256]{1,0:T(8,128)} %refs_5_.1), custom_call_target="tpu_custom_call" | custom-call | flops 9699999744 | bytes 2000000 | tf_op jit(solution)/shard_map/pallas_call | solution.py:513
  43.7 2.3 %shard_map.128 = (f32[1,192]{1,0:T(1,128)}, f32[192,256]{1,0:T(8,128)}, f32[1,192]{1,0:T(1,128)}, f32[192,256]{1,0:T(8,128)}, f32[1,192]{1,0:T(1,128)}, /*index=5*/f32[192,256]{1,0:T(8,128)}) custom-call(f32[1,192]{1,0:T(1,128)} %bitcast.7, f32[192,256]{1,0:T(8,128)} %refs_1_.1, f32[1,192]{1,0:T(1,128)} %bitcast.9, f32[192,256]{1,0:T(8,128)} %refs_3_.1, ...), custom_call_target="tpu_custom_call" | custom-call | tf_op jit(solution)/shard_map/pallas_call | solution.py:565

commit v4 on v3

--- a/solution.py
+++ b/solution.py
@@ -20,8 +20,8 @@
 PLANES = (0, ROWS, 2 * ROWS, 3 * ROWS + 16)
 VECTORS = slice(3 * ROWS, 3 * ROWS + 16)
 BLOCK = 4 * ROWS + 16
-SPLIT = PLANES[3]
-CUT = 288
+SPLIT = 656
+CUT = 320
 OFFSETS = (0, 1, 3, 2)
 COUNT = 128
 GRANT = 62 << 20
@@ -92,25 +92,21 @@
     loads,
 ):
     row, col = lax.axis_index("row"), lax.axis_index("col")
-    z, y = row // RING, row % RING
-    x, c = col // 2, col % 2
+    z, y = lax.div(row, RING), lax.rem(row, RING)
+    x, c = lax.div(col, 2), lax.rem(col, 2)
     o = 1 - c
 
+    def turn(place, d):
+        return lax.rem(place + d, RING)
+
     def first(d):
-        return (z * RING + (y + d) % RING, col)
+        return (z * RING + turn(y, d), col)
 
     def second(d, core):
-        return (((z + o * d) % RING) * RING + y, ((x + c * d) % RING) * 2 + core)
+        return (turn(z, o * d) * RING + y, turn(x, c * d) * 2 + core)
 
     def third(d, core):
-        return (((z + c * d) % RING) * RING + y, ((x + o * d) % RING) * 2 + core)
-
-    barrier = pltpu.get_barrier_semaphore()
-    near = [first(1), first(3), second(1, c), second(3, c)]
-    near += [third(t, c) for t in (1, 2, 3)] + [third(t, o) for t in range(RING)]
-    near += [second(t, o) for t in (1, 2, 3)]
-    for peer in near:
-        pl.semaphore_signal(barrier, inc=1, device_id=peer, device_id_type=MESH)
+        return (turn(z, c * d) * RING + y, turn(x, o * d) * 2 + core)
 
     pairs = (
         (points_hbm, points_ref),
@@ -123,6 +119,14 @@
     arrivals = [pltpu.make_async_copy(a, b, loads.at[i]) for i, (a, b) in enumerate(pairs)]
     for arrival in arrivals:
         arrival.start()
+
+    barrier = pltpu.get_barrier_semaphore()
+    near = [first(1), first(3), second(1, c), second(3, c)]
+    near += [third(t, c) for t in (1, 2, 3)] + [third(t, o) for t in range(RING)]
+    near += [second(t, o) for t in (1, 2, 3)]
+    for peer in near:
+        pl.semaphore_signal(barrier, inc=1, device_id=peer, device_id_type=MESH)
+
     for arrival in arrivals[:4]:
         arrival.wait()
 
@@ -445,13 +449,13 @@
     me = row * 8 + col
 
     def spread(i, carry):
-        peer = (me + i) % COUNT
+        peer = lax.rem(me + i, COUNT)
         pltpu.make_async_remote_copy(
             src_ref=mine,
             dst_ref=arb.at[me],
             send_sem=a_send,
             recv_sem=a_recv,
-            device_id=(peer // 8, peer % 8),
+            device_id=(lax.div(peer, 8), lax.rem(peer, 8)),
             device_id_type=MESH,
         ).start()
         return carry

time: 46.1 us -> 45.3 us (0.983)
  Pallas kernels: 45.3 us -> 44.5 us
    pallas_call x1, Pallas kernels: 43 us -> 42.2 us  [body(): pl.pallas_call(kernel, out_shape=(line, block, jax.ShapeDtypeStruct((1, L...]
where the time goes in v4:
time: 45.3 us; the launch traced here: 45.2 us
  Pallas kernels  44.5 us (98%)
  between operations  0.64 us (1%)
    pallas_call x1, Pallas kernels, body(): pl.pallas_call(kernel, out_shape=(line, block, jax.ShapeDtypeStruct((1, L...  42.2 us
    pallas_call x1, Pallas kernels, body(): pl.pallas_call(update, out_shape=(line, block) * 3, in_specs=[hbm] * 9, o...  2.33 us

profile of v4, /device:TPU:1, one launch (start us, length us, event | category | flops | bytes accessed | tf_op | source)
XLA Modules:
  0.0 45.2 jit_solution(14281779974372222761)
XLA Ops:
  0.6 42.2 %shard_map.127 = (f32[1,192]{1,0:T(1,128)}, f32[192,256]{1,0:T(8,128)}, f32[1,128]{1,0:T(1,128)}) custom-call(bf16[192,256]{1,0:T(8,128)(2,1)} %points_hbm.1, f32[1,256]{1,0:T(1,128)} %bitcast.12, f32[1,192]{1,0:T(1,128)} %bitcast.8, f32[192,256]{1,0:T(8,128)} %refs_3_.1, f32[1,192]{1,0:T(1,128)} %bitcast.10, f32[192,256]{1,0:T(8,128)} %refs_5_.1), custom_call_target="tpu_custom_call" | custom-call | flops 9699999744 | bytes 2000000 | tf_op jit(solution)/shard_map/pallas_call | solution.py:517
  42.8 2.3 %shard_map.128 = (f32[1,192]{1,0:T(1,128)}, f32[192,256]{1,0:T(8,128)}, f32[1,192]{1,0:T(1,128)}, f32[192,256]{1,0:T(8,128)}, f32[1,192]{1,0:T(1,128)}, /*index=5*/f32[192,256]{1,0:T(8,128)}) custom-call(f32[1,192]{1,0:T(1,128)} %bitcast.7, f32[192,256]{1,0:T(8,128)} %refs_1_.1, f32[1,192]{1,0:T(1,128)} %bitcast.9, f32[192,256]{1,0:T(8,128)} %refs_3_.1, ...), custom_call_target="tpu_custom_call" | custom-call | tf_op jit(solution)/shard_map/pallas_call | solution.py:569

commit v5 on v4

--- a/solution.py
+++ b/solution.py
@@ -20,8 +20,8 @@
 PLANES = (0, ROWS, 2 * ROWS, 3 * ROWS + 16)
 VECTORS = slice(3 * ROWS, 3 * ROWS + 16)
 BLOCK = 4 * ROWS + 16
-SPLIT = 656
-CUT = 320
+SPLIT = 688
+CUT = 336
 OFFSETS = (0, 1, 3, 2)
 COUNT = 128
 GRANT = 62 << 20

time: 45.3 us -> 45.7 us (level)
  no operation moved by 1% of the time
where the time goes in v5:
time: 45.7 us; the launch traced here: 45.5 us
  Pallas kernels  44.9 us (98%)
  between operations  0.64 us (1%)
    pallas_call x1, Pallas kernels, body(): pl.pallas_call(kernel, out_shape=(line, block, jax.ShapeDtypeStruct((1, L...  42.6 us
    pallas_call x1, Pallas kernels, body(): pl.pallas_call(update, out_shape=(line, block) * 3, in_specs=[hbm] * 9, o...  2.33 us

profile of v5, /device:TPU:1, one launch (start us, length us, event | category | flops | bytes accessed | tf_op | source)
XLA Modules:
  0.0 45.5 jit_solution(15774645007469470519)
XLA Ops:
  0.6 42.6 %shard_map.127 = (f32[1,192]{1,0:T(1,128)}, f32[192,256]{1,0:T(8,128)}, f32[1,128]{1,0:T(1,128)}) custom-call(bf16[192,256]{1,0:T(8,128)(2,1)} %points_hbm.1, f32[1,256]{1,0:T(1,128)} %bitcast.12, f32[1,192]{1,0:T(1,128)} %bitcast.8, f32[192,256]{1,0:T(8,128)} %refs_3_.1, f32[1,192]{1,0:T(1,128)} %bitcast.10, f32[192,256]{1,0:T(8,128)} %refs_5_.1), custom_call_target="tpu_custom_call" | custom-call | flops 9699999744 | bytes 2000000 | tf_op jit(solution)/shard_map/pallas_call | solution.py:517
  43.2 2.3 %shard_map.128 = (f32[1,192]{1,0:T(1,128)}, f32[192,256]{1,0:T(8,128)}, f32[1,192]{1,0:T(1,128)}, f32[192,256]{1,0:T(8,128)}, f32[1,192]{1,0:T(1,128)}, /*index=5*/f32[192,256]{1,0:T(8,128)}) custom-call(f32[1,192]{1,0:T(1,128)} %bitcast.7, f32[192,256]{1,0:T(8,128)} %refs_1_.1, f32[1,192]{1,0:T(1,128)} %bitcast.9, f32[192,256]{1,0:T(8,128)} %refs_3_.1, ...), custom_call_target="tpu_custom_call" | custom-call | tf_op jit(solution)/shard_map/pallas_call | solution.py:569
